TPU v7x, 32 devices: a whole 2x2x4 slice. The times are simulated.
32 devices in a mesh: groups: 2 (over y), vocab: 16 (over z, x, core).
Axes of the slice: x: 2, y: 2, z: 4, core: 2. Of those that a mesh axis runs over, the one named last changes fastest.
Arguments:
- hidden: bfloat16 [512, 4608], P(('groups', 'vocab')), parts along dimension 0, may hold values from -6 to 6
- weight: bfloat16 [8192, 4608], P('vocab'), may hold values from -0.1875 to 0.1875
- log_totals: float32 [512], P('groups'), parts along dimension 0, may hold values from 4 to 6
- token_cotangent: float32 [512], P('groups'), parts along dimension 0, may hold values from 0.25 to 2
- targets: int32 [512], P('groups'), parts along dimension 0, may hold values from 0 to 8191
- block_list: int32 [128, 2], P(('groups', 'vocab')), parts along dimension 0, may hold values from 0 to 1, as said below
- block_valid: int32 [128], P(('groups', 'vocab')), parts along dimension 0, may hold values from 0 to 1, as said below
Outputs:
- grad_hidden: bfloat16 [512, 4608], P(('groups', 'vocab')), parts along dimension 0
- grad_weight: bfloat16 [16384, 4608], P(('groups', 'vocab')), parts along dimension 0
There are 2 independent parts, one for each index of `groups`. A program takes and returns all parts, laid end to end along the dimension named above; an argument that names none is the same for every part. Nothing has to cross between parts.
Inputs may be any that keep to these rules, and one draw needn't show every extreme that they name: `block_list`: entries s * 4 to s * 4 + 3 belong to vocabulary shard s. Column 0 is a token block below 2, column 1 a vocabulary block below 2; the pairs of one shard are all distinct. `block_valid`: the used entries of a shard come first; every shard uses at least one, and at least one shard uses all 4.
All inputs are finite; a program needn't handle non-finite values.
Results may differ from a plain program's by a relative error of at most 0.0067.
Values may be sent and summed in bfloat16 or wider, within the bound.
A program may use at most 128 MiB of HBM per device.

v0:
```python
import jax
import jax.numpy as jnp
from jax import lax
from jax.sharding import PartitionSpec as P

TB = 128
VB = 256


def take_rows(source, start, count):
    return lax.dynamic_slice_in_dim(source, start, count, 0)


def add_rows(target, start, term):
    current = lax.dynamic_slice_in_dim(target, start, term.shape[0], 0)
    return lax.dynamic_update_slice_in_dim(target, current + term, start, 0)


def block_gradient(rows_hidden, columns, totals, cotangent, labels, first_column):
    logits = jnp.dot(rows_hidden, columns.T, preferred_element_type=jnp.float32)
    column_ids = first_column + lax.broadcasted_iota(jnp.int32, (1, columns.shape[0]), 1)
    target_hit = (labels[:, None] == column_ids).astype(jnp.float32)
    return (cotangent[:, None] * (jnp.exp(logits - totals[:, None]) - target_hit)).astype(
        jnp.bfloat16
    )


def local(hidden, weight, log_totals, token_cotangent, targets, block_list, block_valid):
    gathered = lax.all_gather(hidden, "vocab", axis=0, tiled=True)
    my_index = lax.axis_index("vocab")
    vocab_rows = weight.shape[0]
    tokens = gathered.shape[0]
    features = gathered.shape[1]
    entries = block_list.shape[0]
    first_own = my_index * vocab_rows
    token_index = block_list[:, 0]
    vocab_index = block_list[:, 1]
    grad_rows = jnp.zeros((tokens, features), jnp.float32)
    grad_cols = jnp.zeros((vocab_rows, features), jnp.float32)
    keep_entry = block_valid > 0

    def own_entry(position, carry):

        def compute_entry(carried):
            row_acc, column_acc = carried
            token_start = token_index[position] * TB
            vocab_start = vocab_index[position] * VB
            rows_hidden = take_rows(gathered, token_start, TB)
            columns = take_rows(weight, vocab_start, VB)
            gradient = block_gradient(
                rows_hidden,
                columns,
                take_rows(log_totals, token_start, TB),
                take_rows(token_cotangent, token_start, TB),
                take_rows(targets, token_start, TB),
                first_own + vocab_start,
            )
            column_acc = add_rows(
                column_acc,
                vocab_start,
                jnp.dot(gradient.T, rows_hidden, preferred_element_type=jnp.float32),
            )
            return (row_acc, column_acc)

        return lax.cond(keep_entry[position], compute_entry, lambda carried: carried, carry)

    grad_rows, grad_cols = lax.fori_loop(0, entries, own_entry, (grad_rows, grad_cols))
    start = jnp.int32(0)
    count = lax.axis_size("vocab") * hidden.shape[0]
    sub_hidden = take_rows(gathered, start, count)
    sub_totals = take_rows(log_totals, start, count)
    sub_weights = take_rows(token_cotangent, start, count)
    sub_labels = take_rows(targets, start, count)
    row_block = lax.broadcasted_iota(jnp.int32, (count, 1), 0) // TB

    def entry_rows(position, running):
        token_block = token_index[position]
        meets = (
            keep_entry[position]
            & (token_block * TB < start + count)
            & (token_block * TB + TB > start)
        )

        def compute_rows(carried):
            vocab_start = vocab_index[position] * VB
            columns = take_rows(weight, vocab_start, VB)
            gradient = block_gradient(
                sub_hidden, columns, sub_totals, sub_weights, sub_labels, first_own + vocab_start
            )
            gradient = jnp.where(row_block == token_block, gradient, jnp.zeros_like(gradient))
            return carried + jnp.dot(gradient, columns, preferred_element_type=jnp.float32)

        return lax.cond(meets, compute_rows, lambda carried: carried, running)

    grad_part = lax.psum_scatter(
        lax.fori_loop(0, entries, entry_rows, take_rows(grad_rows, start, count)),
        "vocab",
        scatter_dimension=0,
        tiled=True,
    )
    return (grad_part.astype(jnp.bfloat16), grad_cols.astype(jnp.bfloat16))


def solution(mesh):
    placed = (
        P(("groups", "vocab"), None),
        P("vocab", None),
        P("groups"),
        P("groups"),
        P("groups"),
        P(("groups", "vocab"), None),
        P(("groups", "vocab")),
    )
    return jax.shard_map(
        local,
        mesh=mesh,
        in_specs=placed,
        out_specs=(P(("groups", "vocab"), None), P(("groups", "vocab"), None)),
        check_vma=False,
    )
```

profile of v0, /device:TPU:0, one launch (start us, length us, event | category | flops | bytes accessed | tf_op | source)
XLA Modules:
  0.0 192.8 jit_solution(17176003372691232935)
XLA Ops:
  7.2 0.7 all-gather.2.cloned.1.call-update
  8.0 0.7 broadcast_compare_fusion
  8.6 0.8 slice_bitcast_fusion
  9.4 46.0 %all-gather.2.cloned.1.call-done = bf16[256,4608]{1,0:T(8,128)(2,1)} async-done(((bf16[16,4608]{1,0:T(8,128)(2,1)}), bf16[256,4608]{1,0:T(8,128)(2,1)}) %all-gather.2.cloned.1.call-update) | async-done | bytes 2359312 | tf_op jit(solution)/shard_map/all_gather | solution.py:29
  55.4 2.8 %broadcast_in_dim.22 = f32[256,4608]{1,0:T(8,128)} broadcast(f32[]{:T(128)} %constant.101.clone.1), dimensions={} | broadcast | bytes 4718596 | tf_op jit(solution)/shard_map/broadcast_in_dim | solution.py:38
  58.1 41.3 %while.34 = (s32[]{:T(128)}, f32[256,4608]{1,0:T(8,128)}, pred[4]{0:T(512)(128)(4,1)S(1)}, s32[4]{0:T(128)S(1)}, f32[256]{0:T(256)S(1)}, /*index=5*/s32[4]{0:T(1...) while((s32[]{:T(128)}, f32[256,4608]{1,0:T(8,128)}, ...), condition=%wide.region_3.0_spmd.clone, body=%wide.region_0.0_spmd.clone.sunk | while | flops 1209600512 | bytes 16528340 | solution.py:96
  58.2 0.6 dynamic_slice.98
  59.3 0.6 dynamic_slice.97
  60.6 10.5 %conditional.6 = (f32[256,4608]{1,0:T(8,128)}) conditional(s32[]{:T(128)} %convert_element_type.60, f32[256,4608]{1,0:T(8,128)} %get-tuple-element.736, (s32[]{:T(128)}, s32[256,1]{0,1:T(1,128)S(1)}, f32[256]{0:T(256)S(1)}, s32[]{:T(128)}, s32[4]{0:T(128)S(1)}, /*index=5*/bf16[512,4608]{1,0:T(8,128)(2,1)}, bf16[256,4608]{1,0:T(8,128)(2,1)S(1)}, ...), branch_computations={%region_1.0_spmd, %region_2.0_spmd.clone} | conditional | flops 1209600256 | bytes 16525952 | solution.py:93
  60.6 0.6 dynamic_slice.53
  61.8 0.6 compare_reduce_fusion
  62.4 8.7 %convolution_add_fusion.1 = f32[256,4608]{1,0:T(8,128)} fusion(f32[256,4608]{1,0:T(8,128)} %get-tuple-element.508, bf16[512,4608]{1,0:T(8,128)(2,1)} %get-tuple-element.511, s32[]{:T(128)S(6)} %select_n.56, bf16[256,4608]{1,0:T(8,128)(2,1)S(1)} %get-tuple-element.514, s32[256]{0:T(256)S(1)} %iota_add_fusion.1, f32[256]{0:T(256)S(1)} %get-tuple-element.515, ...), kind=kOutput, calls=%fused_computation.19 | convolution fusion | flops 1209597952 | bytes 16520448 | tf_op jit(solution)/shard_map/while/body/eval_jaxpr/cond/branch_1_fun/dot_general | solution.py:91
  71.1 0.6 dynamic_slice.98
  72.3 0.6 dynamic_slice.97
  73.6 10.5 %conditional.6 = (f32[256,4608]{1,0:T(8,128)}) conditional(s32[]{:T(128)} %convert_element_type.60, f32[256,4608]{1,0:T(8,128)} %get-tuple-element.736, (s32[]{:T(128)}, s32[256,1]{0,1:T(1,128)S(1)}, f32[256]{0:T(256)S(1)}, s32[]{:T(128)}, s32[4]{0:T(128)S(1)}, /*index=5*/bf16[512,4608]{1,0:T(8,128)(2,1)}, bf16[256,4608]{1,0:T(8,128)(2,1)S(1)}, ...), branch_computations={%region_1.0_spmd, %region_2.0_spmd.clone} | conditional | flops 1209600256 | bytes 16525952 | solution.py:93
  73.6 0.6 dynamic_slice.53
  74.8 0.6 compare_reduce_fusion
  75.4 8.7 %convolution_add_fusion.1 = f32[256,4608]{1,0:T(8,128)} fusion(f32[256,4608]{1,0:T(8,128)} %get-tuple-element.508, bf16[512,4608]{1,0:T(8,128)(2,1)} %get-tuple-element.511, s32[]{:T(128)S(6)} %select_n.56, bf16[256,4608]{1,0:T(8,128)(2,1)S(1)} %get-tuple-element.514, s32[256]{0:T(256)S(1)} %iota_add_fusion.1, f32[256]{0:T(256)S(1)} %get-tuple-element.515, ...), kind=kOutput, calls=%fused_computation.19 | convolution fusion | flops 1209597952 | bytes 16520448 | tf_op jit(solution)/shard_map/while/body/eval_jaxpr/cond/branch_1_fun/dot_general | solution.py:91
  84.0 0.6 dynamic_slice.98
  85.2 0.6 dynamic_slice.97
  86.5 10.5 %conditional.6 = (f32[256,4608]{1,0:T(8,128)}) conditional(s32[]{:T(128)} %convert_element_type.60, f32[256,4608]{1,0:T(8,128)} %get-tuple-element.736, (s32[]{:T(128)}, s32[256,1]{0,1:T(1,128)S(1)}, f32[256]{0:T(256)S(1)}, s32[]{:T(128)}, s32[4]{0:T(128)S(1)}, /*index=5*/bf16[512,4608]{1,0:T(8,128)(2,1)}, bf16[256,4608]{1,0:T(8,128)(2,1)S(1)}, ...), branch_computations={%region_1.0_spmd, %region_2.0_spmd.clone} | conditional | flops 1209600256 | bytes 16525952 | solution.py:93
  86.5 0.6 dynamic_slice.53
  87.7 0.6 compare_reduce_fusion
  88.3 8.7 %convolution_add_fusion.1 = f32[256,4608]{1,0:T(8,128)} fusion(f32[256,4608]{1,0:T(8,128)} %get-tuple-element.508, bf16[512,4608]{1,0:T(8,128)(2,1)} %get-tuple-element.511, s32[]{:T(128)S(6)} %select_n.56, bf16[256,4608]{1,0:T(8,128)(2,1)S(1)} %get-tuple-element.514, s32[256]{0:T(256)S(1)} %iota_add_fusion.1, f32[256]{0:T(256)S(1)} %get-tuple-element.515, ...), kind=kOutput, calls=%fused_computation.19 | convolution fusion | flops 1209597952 | bytes 16520448 | tf_op jit(solution)/shard_map/while/body/eval_jaxpr/cond/branch_1_fun/dot_general | solution.py:91
  97.0 0.6 dynamic_slice.98
  98.2 0.6 dynamic_slice.97
  99.5 4.8 %broadcast_in_dim.23 = f32[512,4608]{1,0:T(8,128)} broadcast(f32[]{:T(128)} %constant.101.clone.1), dimensions={} | broadcast | bytes 9437188 | tf_op jit(solution)/shard_map/broadcast_in_dim | solution.py:39
  104.3 37.7 %while.33 = (s32[]{:T(128)}, f32[512,4608]{1,0:T(8,128)}, pred[4]{0:T(512)(128)(4,1)S(1)}, s32[4]{0:T(128)S(1)}, s32[4]{0:T(128)S(1)}, /*index=5*/f32[256]{0:T(2...) while((s32[]{:T(128)}, f32[512,4608]{1,0:T(8,128)}, ...), condition=%wide.region_8.9_spmd, body=%wide.region_5.8_spmd.sunk | while | flops 605356288 | bytes 14164874 | solution.py:67
  104.3 0.6 dynamic_slice.96
  105.5 10.7 %conditional.5 = (f32[512,4608]{1,0:T(8,128)}) conditional(s32[]{:T(128)} %bitcast.28, f32[512,4608]{1,0:T(8,128)} %get-tuple-element.778, (s32[]{:T(128)}, s32[4]{0:T(128)S(1)}, f32[512,4608]{1,0:T(8,128)}, s32[4]{0:T(128)S(1)}, f32[256]{0:T(256)S(1)}, /*index=5*/bf16[256,4608]{1,0:T(8,128)(2,1)S(1)}, bf16[512,4608]{1,0:T(8,128)(2,1)}, ...), branch_computations={%region_6.6_spmd, %region_7.7_spmd} | conditional | flops 605356288 | bytes 14164666 | solution.py:65
  105.6 0.6 dynamic_slice.44
  106.8 0.1 dynamic_slice.45
  107.0 0.6 dynamic_slice.42
  108.3 8.0 %fusion.2 = f32[512,4608]{1,0:T(8,128)} fusion(f32[512,4608]{1,0:T(8,128)} %get-tuple-element.438, s32[]{:T(128)S(6)} %select_n.46, bf16[512,4608]{1,0:T(8,128)(2,1)} %get-tuple-element.444, bf16[256,4608]{1,0:T(8,128)(2,1)S(1)} %get-tuple-element.443, s32[]{:T(128)S(6)} %select_n.47, s32[256]{0:T(256)S(1)} %iota_add_fusion, f32[128]{0:T(128)S(1)} %dynamic_slice.48, ...), kind=kOutput, calls=%fused_computation.2 | convolution fusion | flops 605356032 | bytes 14160384 | tf_op jit(solution)/shard_map/while/body/eval_jaxpr/cond/branch_1_fun/dot_general | solution.py:61
  116.3 0.6 dynamic_slice.96
  117.5 11.2 %conditional.5 = (f32[512,4608]{1,0:T(8,128)}) conditional(s32[]{:T(128)} %bitcast.28, f32[512,4608]{1,0:T(8,128)} %get-tuple-element.778, (s32[]{:T(128)}, s32[4]{0:T(128)S(1)}, f32[512,4608]{1,0:T(8,128)}, s32[4]{0:T(128)S(1)}, f32[256]{0:T(256)S(1)}, /*index=5*/bf16[256,4608]{1,0:T(8,128)(2,1)S(1)}, bf16[512,4608]{1,0:T(8,128)(2,1)}, ...), branch_computations={%region_6.6_spmd, %region_7.7_spmd} | conditional | flops 605356288 | bytes 14164666 | solution.py:65
  117.6 0.6 dynamic_slice.44
  119.0 0.6 dynamic_slice.42
  120.3 8.4 %fusion.2 = f32[512,4608]{1,0:T(8,128)} fusion(f32[512,4608]{1,0:T(8,128)} %get-tuple-element.438, s32[]{:T(128)S(6)} %select_n.46, bf16[512,4608]{1,0:T(8,128)(2,1)} %get-tuple-element.444, bf16[256,4608]{1,0:T(8,128)(2,1)S(1)} %get-tuple-element.443, s32[]{:T(128)S(6)} %select_n.47, s32[256]{0:T(256)S(1)} %iota_add_fusion, f32[128]{0:T(128)S(1)} %dynamic_slice.48, ...), kind=kOutput, calls=%fused_computation.2 | convolution fusion | flops 605356032 | bytes 14160384 | tf_op jit(solution)/shard_map/while/body/eval_jaxpr/cond/branch_1_fun/dot_general | solution.py:61
  128.7 0.6 dynamic_slice.96
  129.9 10.8 %conditional.5 = (f32[512,4608]{1,0:T(8,128)}) conditional(s32[]{:T(128)} %bitcast.28, f32[512,4608]{1,0:T(8,128)} %get-tuple-element.778, (s32[]{:T(128)}, s32[4]{0:T(128)S(1)}, f32[512,4608]{1,0:T(8,128)}, s32[4]{0:T(128)S(1)}, f32[256]{0:T(256)S(1)}, /*index=5*/bf16[256,4608]{1,0:T(8,128)(2,1)S(1)}, bf16[512,4608]{1,0:T(8,128)(2,1)}, ...), branch_computations={%region_6.6_spmd, %region_7.7_spmd} | conditional | flops 605356288 | bytes 14164666 | solution.py:65
  130.0 0.6 dynamic_slice.44
  131.4 0.6 dynamic_slice.42
  132.7 8.0 %fusion.2 = f32[512,4608]{1,0:T(8,128)} fusion(f32[512,4608]{1,0:T(8,128)} %get-tuple-element.438, s32[]{:T(128)S(6)} %select_n.46, bf16[512,4608]{1,0:T(8,128)(2,1)} %get-tuple-element.444, bf16[256,4608]{1,0:T(8,128)(2,1)S(1)} %get-tuple-element.443, s32[]{:T(128)S(6)} %select_n.47, s32[256]{0:T(256)S(1)} %iota_add_fusion, f32[128]{0:T(128)S(1)} %dynamic_slice.48, ...), kind=kOutput, calls=%fused_computation.2 | convolution fusion | flops 605356032 | bytes 14160384 | tf_op jit(solution)/shard_map/while/body/eval_jaxpr/cond/branch_1_fun/dot_general | solution.py:61
  140.7 0.6 dynamic_slice.96
  142.0 6.4 %convert_element_type.36 = bf16[512,4608]{1,0:T(8,128)(2,1)} convert(f32[512,4608]{1,0:T(8,128)} %get-tuple-element.465) | non-fusion elementwise | flops 2359296 | bytes 14155776 | tf_op jit(solution)/shard_map/convert_element_type | solution.py:101
  148.3 36.0 %reduce-scatter.2.cloned.1.call-done = f32[16,4608]{1,0:T(8,128)} async-done(((f32[256,4608]{1,0:T(8,128)}), f32[16,4608]{1,0:T(8,128)}) %reduce-scatter.2.cloned.1.call-update) | async-done | bytes 294928 | tf_op jit(solution)/shard_map/reduce_scatter | solution.py:95
  184.3 1.6 convert_element_type.35
  (35 shorter events, 0.8 us)
Async XLA Ops:
  7.2 51.0 %copy-start.2 = (f32[256]{0:T(256)S(1)}, f32[256]{0:T(256)}, u32[]{:S(2)}) copy-start(f32[256]{0:T(256)} %param.17) | copy-start | bytes 3076
  7.2 51.0 %copy-start.1 = (f32[256]{0:T(256)S(1)}, f32[256]{0:T(256)}, u32[]{:S(2)}) copy-start(f32[256]{0:T(256)} %param.18) | copy-start | bytes 3076
  7.2 51.0 %copy-start.3 = (s32[256]{0:T(256)S(1)}, s32[256]{0:T(256)}, u32[]{:S(2)}) copy-start(s32[256]{0:T(256)} %param.19) | copy-start | bytes 3076
  7.2 48.2 %all-gather.2.cloned.1.call-start = ((), (), s32[]{:S(2)}) async-start(), calls=%async_computation.1 | async-start | bytes 2506752 | tf_op jit(solution)/shard_map/all_gather | solution.py:29
  7.9 176.4 %reduce-scatter.2.cloned.1.call-start = ((), (), s32[]{:S(2)}) async-start(), calls=%async_computation.2 | async-start | bytes 5013504 | tf_op jit(solution)/shard_map/reduce_scatter | solution.py:95
  55.4 2.8 %copy-start = (bf16[256,4608]{1,0:T(8,128)(2,1)S(1)}, bf16[256,4608]{1,0:T(8,128)(2,1)}, u32[]{:S(2)}) copy-start(bf16[256,4608]{1,0:T(8,128)(2,1)} %all-gather.2.cloned.1.call-done) | copy-start | bytes 7077892
Sparse Core Ops, SparseCore 0:
  10.3 45.0 all-gather.1
  99.6 84.6 reduce-scatter.1
where the time goes:
time: 193 us
  waiting for transfers between devices  82.7 us (43%)
  matrix products  50.4 us (26%)
  local copies, waits for them, and re-layouts  21.5 us (11%)
  between operations  14.1 us (7%)
  loops' own time  13.6 us (7%)
  other arithmetic  10.5 us (5%)
    all_gather x1, waiting for transfers between devices, local(): gathered = lax.all_gather(hidden, 'vocab', axis=0, tiled=True)  46 us
    reduce_scatter x1, waiting for transfers between devices, local(): lax.psum_scatter(lax.fori_loop(0, entries, entry_rows, take_rows(grad_row...  36 us
    dot_general x3, matrix products, compute_rows(): jnp.dot(gradient, columns, preferred_element_type=jnp.float32)  26 us
    dot_general x3, matrix products, compute_entry(): jnp.dot(gradient.T, rows_hidden, preferred_element_type=jnp.float32)  24.4 us
    convert_element_type x2, other arithmetic, local(): return (grad_part.astype(jnp.bfloat16), grad_cols.astype(jnp.bfloat16))  8.01 us
    another operation x1, loops' own time, local(): lax.fori_loop(0, entries, entry_rows, take_rows(grad_rows, start, count))  4.99 us
    broadcast_in_dim x1, local copies, waits for them, and re-layouts, local(): grad_cols = jnp.zeros((vocab_rows, features), jnp.float32)  4.8 us
    another operation x4, loops' own time, own_entry(): lax.cond(keep_entry[position], compute_entry, lambda carried: carried, ca...  4.07 us
  transfers between devices with their start and end apart: 2, of which 2 were waited for; matrix products, arithmetic and copies ran while one was open for 23% of the time, Pallas kernels for 0%

commit v1 on v0

--- a/solution.py
+++ b/solution.py
@@ -1,6 +1,8 @@
 import jax
 import jax.numpy as jnp
 from jax import lax
+from jax.experimental import pallas as pl
+from jax.experimental.pallas import tpu as pltpu
 from jax.sharding import PartitionSpec as P
 
 TB = 128
@@ -101,6 +103,253 @@
     return (grad_part.astype(jnp.bfloat16), grad_cols.astype(jnp.bfloat16))
 
 
+NZ, NX, NC = 4, 2, 2
+CHUNK = 16
+GROUP = NX * NC * CHUNK
+HALVES = 2
+GATHER_ORDER = (0, 1, 3, 2)
+SCATTER_ORDER = (2, 1, 3, 0)
+MESH = pl.DeviceIdType.MESH
+
+
+def head_kernel(
+    hidden, weight, totals, cotangent, labels, entry_list, entry_valid,
+    grad_hidden, gradient_out, gathered_out,
+    rows, head, grad, part, totals_col, cotangent_col, labels_col,
+    core_out, core_in, core_own, x_out, x_in, x_own, z_out, z_in,
+    gz_send, gz_recv, gx_send, gx_recv, gc_send, gc_recv,
+    sc_send, sc_recv, sx_send, sx_recv, sz_send, sz_recv, local_sem,
+):
+    me = lax.axis_index("vocab")
+    core = lax.rem(me, NC)
+    x = lax.rem(me // NC, NX)
+    z = me // (NX * NC)
+    vocab_rows, features = head.shape
+    width = features // HALVES
+
+    def index(z_, x_, c_):
+        return z_ * (NX * NC) + x_ * NC + c_
+
+    def plane(k):
+        return lax.rem(z + k, NZ)
+
+    def chunk(device):
+        return pl.ds(pl.multiple_of(device * CHUNK, CHUNK), CHUNK)
+
+    def piece(offset):
+        return pl.ds(pl.multiple_of(offset, CHUNK), CHUNK)
+
+    def remote(source, target, send, recv, device):
+        return pltpu.make_async_remote_copy(
+            src_ref=source, dst_ref=target, send_sem=send, recv_sem=recv,
+            device_id={"vocab": device}, device_id_type=MESH,
+        )
+
+    core_peer = index(z, x, 1 - core)
+    x_peer = index(z, 1 - x, core)
+    z_peers = [index(plane(k), x, core) for k in range(1, NZ)]
+
+    load_head = pltpu.make_async_copy(weight, head, local_sem.at[0])
+    load_rows = pltpu.make_async_copy(hidden, rows.at[chunk(me)], local_sem.at[1])
+    load_rows.start()
+    load_head.start()
+
+    barrier = pltpu.get_barrier_semaphore()
+    for peer in [core_peer, x_peer] + z_peers:
+        pl.semaphore_signal(barrier, inc=1, device_id={"vocab": peer}, device_id_type=MESH)
+
+    for vector, column in (
+        (totals, totals_col), (cotangent, cotangent_col), (labels, labels_col)
+    ):
+        column[...] = jnp.broadcast_to(vector[...], (128, vector.shape[1])).T
+
+    load_rows.wait()
+    pl.semaphore_wait(barrier, NZ + 1)
+
+    def gather_copy(source, send, recv, device):
+        held = rows.at[chunk(source)]
+        return remote(held, held, send, recv, device)
+
+    gather_z = {
+        k: gather_copy(me, gz_send.at[k], gz_recv.at[k], index(lax.rem(z + NZ - k, NZ), x, core))
+        for k in range(1, NZ)
+    }
+    gather_x = {
+        k: gather_copy(index(plane(k), x, core), gx_send.at[k], gx_recv.at[k], x_peer)
+        for k in range(NZ)
+    }
+    gather_c = {
+        (k, i): gather_copy(
+            index(plane(k), (x, 1 - x)[i], core), gc_send.at[2 * k + i], gc_recv.at[2 * k + i], core_peer
+        )
+        for k in range(NZ)
+        for i in range(NX)
+    }
+    gather_x[0].start()
+    for k in GATHER_ORDER[1:]:
+        gather_z[k].start()
+    gather_c[0, 0].start()
+
+    def dlogits(k):
+        zk = plane(k)
+        span = pl.ds(pl.multiple_of(zk * GROUP, GROUP), GROUP)
+        gather_c[k, 0].wait_recv()
+        gather_c[k, 1].wait_recv()
+        logits = lax.dot_general(
+            rows[span, :], head[...], (((1,), (1,)), ((), ())), preferred_element_type=jnp.float32
+        )
+        column = lax.broadcasted_iota(jnp.int32, (1, vocab_rows), 1)
+        token_block = zk * GROUP // TB
+        keep = jnp.zeros((1, vocab_rows), jnp.int32)
+        for e in range(entry_valid.shape[0]):
+            used = jnp.where(
+                (entry_list[e, 0] == token_block) & (entry_valid[e] > 0), entry_list[e, 1], -1
+            )
+            keep = jnp.where(column // VB == used, 1, keep)
+        hit = (labels_col[span, 0:1] == me * vocab_rows + column).astype(jnp.float32)
+        value = cotangent_col[span, 0:1] * (jnp.exp(logits - totals_col[span, 0:1]) - hit)
+        grad[span, :] = jnp.where(keep > 0, value, 0.0).astype(jnp.bfloat16)
+
+    for i, k in enumerate(GATHER_ORDER):
+        if k:
+            gather_z[k].wait_recv()
+            gather_x[k].start()
+            gather_c[k, 0].start()
+        gather_x[k].wait_recv()
+        gather_c[k, 1].start()
+        if i == 0:
+            load_head.wait()
+        else:
+            dlogits(GATHER_ORDER[i - 1])
+    dlogits(GATHER_ORDER[-1])
+
+    save_rows = pltpu.make_async_copy(rows, gathered_out, local_sem.at[2])
+    save_grad = pltpu.make_async_copy(grad, gradient_out, local_sem.at[3])
+    save_rows.start()
+    save_grad.start()
+
+    steps = [(k, h) for k in SCATTER_ORDER for h in range(HALVES)]
+    scatter_c = [
+        remote(core_out.at[s], core_in.at[s], sc_send.at[s], sc_recv.at[s], core_peer)
+        for s in range(len(steps))
+    ]
+    scatter_x = [
+        remote(x_out.at[s], x_in.at[s], sx_send.at[s], sx_recv.at[s], x_peer)
+        for s in range(len(steps))
+    ]
+    scatter_z = {
+        s: remote(
+            z_out.at[s], z_in.at[s], sz_send.at[s], sz_recv.at[s], index(plane(k), x, core)
+        )
+        for s, (k, h) in enumerate(steps)
+        if k
+    }
+
+    def make_part(s):
+        k, h = steps[s]
+        span = pl.ds(pl.multiple_of(plane(k) * GROUP, GROUP), GROUP)
+        part[...] = jnp.dot(
+            grad[span, :], head[:, h * width:(h + 1) * width], preferred_element_type=jnp.float32
+        )
+        for i in range(NX):
+            here = slice(i * CHUNK, (i + 1) * CHUNK)
+            core_out[s, here, :] = part[piece((i * NC + 1 - core) * CHUNK), :].astype(jnp.bfloat16)
+            core_own[s, here, :] = part[piece((i * NC + core) * CHUNK), :]
+        scatter_c[s].start()
+
+    def add_core(s):
+        scatter_c[s].wait_recv()
+        away, own = piece((1 - x) * CHUNK), piece(x * CHUNK)
+        x_out[s] = (core_own[s, away, :] + core_in[s, away, :].astype(jnp.float32)).astype(jnp.bfloat16)
+        scatter_x[s].start()
+        x_own[s] = core_own[s, own, :] + core_in[s, own, :].astype(jnp.float32)
+
+    def add_x(s):
+        scatter_x[s].wait_recv()
+        total = x_own[s] + x_in[s].astype(jnp.float32)
+        if s in scatter_z:
+            z_out[s] = total.astype(jnp.bfloat16)
+            scatter_z[s].start()
+        else:
+            x_own[s] = total
+
+    for s in range(len(steps) + 2):
+        if s < len(steps):
+            make_part(s)
+        if 0 <= s - 1 < len(steps):
+            add_core(s - 1)
+        if 0 <= s - 2 < len(steps):
+            add_x(s - 2)
+
+    for h in range(HALVES):
+        total = x_own[steps.index((0, h))]
+        for s, (k, half) in enumerate(steps):
+            if k and half == h:
+                scatter_z[s].wait_recv()
+                total = total + z_in[s].astype(jnp.float32)
+        grad_hidden[:, h * width:(h + 1) * width] = total.astype(jnp.bfloat16)
+
+    for copy in (
+        list(gather_z.values()) + list(gather_x.values()) + list(gather_c.values())
+        + scatter_c + scatter_x + list(scatter_z.values())
+    ):
+        copy.wait_send()
+    save_rows.wait()
+    save_grad.wait()
+
+
+def local_fused(hidden, weight, log_totals, token_cotangent, targets, block_list, block_valid):
+    tokens = log_totals.shape[0]
+    vocab_rows, features = weight.shape
+    width = features // HALVES
+    steps = NZ * HALVES
+    bf16, f32 = jnp.bfloat16, jnp.float32
+    vmem = pl.BlockSpec(memory_space=pltpu.VMEM)
+    smem = pl.BlockSpec(memory_space=pltpu.SMEM)
+    hbm = pl.BlockSpec(memory_space=pl.ANY)
+    dma = pltpu.SemaphoreType.DMA
+    grad_hidden, gradient, gathered = pl.pallas_call(
+        head_kernel,
+        out_shape=(
+            jax.ShapeDtypeStruct(hidden.shape, bf16),
+            jax.ShapeDtypeStruct((tokens, vocab_rows), bf16),
+            jax.ShapeDtypeStruct((tokens, features), bf16),
+        ),
+        in_specs=[hbm, hbm, vmem, vmem, vmem, smem, smem],
+        out_specs=(vmem, hbm, hbm),
+        scratch_shapes=[
+            pltpu.VMEM((tokens, features), bf16),
+            pltpu.VMEM((vocab_rows, features), bf16),
+            pltpu.VMEM((tokens, vocab_rows), bf16),
+            pltpu.VMEM((GROUP, width), f32),
+            pltpu.VMEM((tokens, 128), f32),
+            pltpu.VMEM((tokens, 128), f32),
+            pltpu.VMEM((tokens, 128), jnp.int32),
+            pltpu.VMEM((steps, NX * CHUNK, width), bf16),
+            pltpu.VMEM((steps, NX * CHUNK, width), bf16),
+            pltpu.VMEM((steps, NX * CHUNK, width), f32),
+            pltpu.VMEM((steps, CHUNK, width), bf16),
+            pltpu.VMEM((steps, CHUNK, width), bf16),
+            pltpu.VMEM((steps, CHUNK, width), f32),
+            pltpu.VMEM((steps, CHUNK, width), bf16),
+            pltpu.VMEM((steps, CHUNK, width), bf16),
+            dma((NZ,)), dma((NZ,)), dma((NZ,)), dma((NZ,)), dma((2 * NZ,)), dma((2 * NZ,)),
+            dma((steps,)), dma((steps,)), dma((steps,)), dma((steps,)), dma((steps,)), dma((steps,)),
+            dma((4,)),
+        ],
+        compiler_params=pltpu.CompilerParams(
+            collective_id=0, has_side_effects=True, vmem_limit_bytes=48 * 1024 * 1024
+        ),
+    )(
+        hidden, weight, log_totals[None, :], token_cotangent[None, :], targets[None, :],
+        block_list, block_valid,
+    )
+    grad_weight = lax.dot_general(
+        gradient, gathered, (((0,), (0,)), ((), ())), preferred_element_type=f32
+    )
+    return (grad_hidden, grad_weight.astype(bf16))
+
+
 def solution(mesh):
     placed = (
         P(("groups", "vocab"), None),
@@ -111,8 +360,9 @@
         P(("groups", "vocab"), None),
         P(("groups", "vocab")),
     )
+    fused = mesh.shape["vocab"] == NZ * NX * NC
     return jax.shard_map(
-        local,
+        local_fused if fused else local,
         mesh=mesh,
         in_specs=placed,
         out_specs=(P(("groups", "vocab"), None), P(("groups", "vocab"), None)),

time: 193 us -> 65.7 us (0.34)
  waiting for transfers between devices: 82.7 us -> 0 us
  Pallas kernels: 0 us -> 56.2 us
  matrix products: 50.4 us -> 3.61 us
  local copies, waits for them, and re-layouts: 21.5 us -> 5.03 us
  loops' own time: 13.6 us -> 0 us
  between operations: 14.1 us -> 0.64 us
  other arithmetic: 10.5 us -> 0 us
    pallas_call x0 -> x1, Pallas kernels: none -> 56.2 us  [local_fused(): pl.pallas_call(head_kernel, out_shape=(jax.ShapeDtypeStruct(hidden.shape,...]
    dot_general x6 -> x1, matrix products: 50.4 us -> 3.61 us  [local_fused(): lax.dot_general(gradient, gathered, (((0,), (0,)), ((), ())), preferred_e...]
    all_gather x1 -> x0, waiting for transfers between devices: 46 us -> none  [local(): gathered = lax.all_gather(hidden, 'vocab', axis=0, tiled=True)]
    reduce_scatter x1 -> x0, waiting for transfers between devices: 36 us -> none  [local(): lax.psum_scatter(lax.fori_loop(0, entries, entry_rows, take_rows(grad_row...]
    another operation x10 -> x0, loops' own time: 13.6 us -> none  [the longest x1 4.99 us: local(): lax.fori_loop(0, entries, entry_rows, take_rows(grad_rows, start, count))]
    dynamic_slice x30 -> x0, local copies, waits for them, and re-layouts: 13.1 us -> none  [the longest x4 2.46 us: entry_rows(): keep_entry[position] & (token_block * TB < start + count)]
    convert_element_type x2 -> x0, other arithmetic: 8.01 us -> none  [local(): return (grad_part.astype(jnp.bfloat16), grad_cols.astype(jnp.bfloat16))]
    broadcast_in_dim x2 -> x0, local copies, waits for them, and re-layouts: 7.56 us -> none  [the longest x1 4.8 us: local(): grad_cols = jnp.zeros((vocab_rows, features), jnp.float32)]
  transfers between devices with their start and end apart: 2 -> 0, of which waited for: 2 -> 0; matrix products, arithmetic and copies ran while one was open for 23% -> 0% of each run, Pallas kernels for 0% -> 0%
where the time goes in v1:
time: 65.7 us; the launch traced here: 65.5 us
  Pallas kernels  56.2 us (86%)
  local copies, waits for them, and re-layouts  5.03 us (8%)
  matrix products  3.61 us (5%)
    pallas_call x1, Pallas kernels, local_fused(): pl.pallas_call(head_kernel, out_shape=(jax.ShapeDtypeStruct(hidden.shape,...  56.2 us
    unnamed x12, local copies, waits for them, and re-layouts  5.03 us
    dot_general x1, matrix products, local_fused(): lax.dot_general(gradient, gathered, (((0,), (0,)), ((), ())), preferred_e...  3.61 us

profile of v1, /device:TPU:0, one launch (start us, length us, event | category | flops | bytes accessed | tf_op | source)
XLA Modules:
  0.0 65.5 jit_solution(17211732566296726779)
XLA Ops:
  0.6 0.8 %copy.9.entry_list = s32[4,2]{1,0:T(4,128)S(1)} copy(s32[4,2]{0,1:T(2,128)} %param.12) | data formatting | bytes 64 | tf_op args[5]
  1.4 0.0 copy-start
  1.4 0.9 %copy-done = bf16[16,4608]{1,0:T(8,128)(2,1)S(1)} copy-done((bf16[16,4608]{1,0:T(8,128)(2,1)S(1)}, bf16[16,4608]{1,0:T(8,128)(2,1)}, u32[]{:S(2)}) %copy-start) | copy-done | bytes 147480
  2.3 0.0 copy-start.1
  2.3 0.7 %copy-done.1 = f32[256]{0:T(256)S(1)} copy-done((f32[256]{0:T(256)S(1)}, f32[256]{0:T(256)}, u32[]{:S(2)}) %copy-start.1) | copy-done | bytes 1048
  3.0 0.0 copy-start.2
  3.0 0.7 %copy-done.2 = f32[256]{0:T(256)S(1)} copy-done((f32[256]{0:T(256)S(1)}, f32[256]{0:T(256)}, u32[]{:S(2)}) %copy-start.2) | copy-done | bytes 1048
  3.7 0.0 copy-start.3
  3.7 0.7 %copy-done.3 = s32[256]{0:T(256)S(1)} copy-done((s32[256]{0:T(256)S(1)}, s32[256]{0:T(256)}, u32[]{:S(2)}) %copy-start.3) | copy-done | bytes 1048
  4.3 0.0 copy-start.4
  4.3 0.7 copy-done.4
  5.0 56.2 %shard_map.86 = (bf16[16,4608]{1,0:T(8,128)(2,1)S(1)}, bf16[256,512]{1,0:T(8,128)(2,1)S(1)}, bf16[256,4608]{1,0:T(8,128)(2,1)S(1)}) custom-call(bf16[16,4608]{1,0:T(8,128)(2,1)S(1)} %copy-done, bf16[512,4608]{1,0:T(8,128)(2,1)} %weight.1, f32[1,256]{1,0:T(1,128)S(1)} %bitcast.5, f32[1,256]{1,0:T(1,128)S(1)} %bitcast.6, s32[1,256]{1,0:T(1,128)S(1)} %bitcast.7, ...), custom_call_target="tpu_custom_call" | custom-call | tf_op jit(solution)/shard_map/pallas_call | solution.py:311
  61.2 3.6 %convolution_convert_fusion = bf16[512,4608]{1,0:T(8,128)(2,1)} fusion(bf16[256,512]{1,0:T(8,128)(2,1)S(1)} %get-tuple-element.6, bf16[256,4608]{1,0:T(8,128)(2,1)S(1)} %get-tuple-element.7), kind=kOutput, calls=%fused_computation | convolution fusion | flops 1210318848 | bytes 7340032 | tf_op jit(solution)/shard_map/dot_general | solution.py:347
  64.8 0.7 %copy.11 = bf16[16,4608]{1,0:T(8,128)(2,1)} copy(bf16[16,4608]{1,0:T(8,128)(2,1)S(1)} %get-tuple-element.10) | data formatting | bytes 294912
Async XLA Ops:
  1.4 0.9 %copy-start = (bf16[16,4608]{1,0:T(8,128)(2,1)S(1)}, bf16[16,4608]{1,0:T(8,128)(2,1)}, u32[]{:S(2)}) copy-start(bf16[16,4608]{1,0:T(8,128)(2,1)} %hidden.1) | copy-start | bytes 442372
  2.3 0.7 %copy-start.1 = (f32[256]{0:T(256)S(1)}, f32[256]{0:T(256)}, u32[]{:S(2)}) copy-start(f32[256]{0:T(256)} %param.9) | copy-start | bytes 3076
  3.0 0.7 %copy-start.2 = (f32[256]{0:T(256)S(1)}, f32[256]{0:T(256)}, u32[]{:S(2)}) copy-start(f32[256]{0:T(256)} %param.10) | copy-start | bytes 3076
  3.7 0.7 %copy-start.3 = (s32[256]{0:T(256)S(1)}, s32[256]{0:T(256)}, u32[]{:S(2)}) copy-start(s32[256]{0:T(256)} %param.11) | copy-start | bytes 3076
  4.3 0.7 %copy-start.4 = (s32[4]{0:T(128)S(1)}, s32[4]{0:T(128)}, u32[]{:S(2)}) copy-start(s32[4]{0:T(128)} %entry_valid.1) | copy-start | bytes 52

commit v2 on v1

--- a/solution.py
+++ b/solution.py
@@ -107,15 +107,17 @@
 CHUNK = 16
 GROUP = NX * NC * CHUNK
 HALVES = 2
-GATHER_ORDER = (0, 1, 3, 2)
-SCATTER_ORDER = (2, 1, 3, 0)
+GATHER_HALVES = 2
+ARRIVALS = ((0, 1, 2, 3), (1, 2, 0, 3), (2, 1, 3, 0), (3, 2, 1, 0))
+SCATTER_ORDER = (1, 3, 2, 0)
 MESH = pl.DeviceIdType.MESH
 
 
 def head_kernel(
     hidden, weight, totals, cotangent, labels, entry_list, entry_valid,
     grad_hidden, gradient_out, gathered_out,
-    rows, head, grad, part, totals_col, cotangent_col, labels_col,
+    rows, head, grad, part, totals_row, cotangent_row, labels_row, list_held, valid_held,
+    totals_col, cotangent_col, labels_col, logits_acc,
     core_out, core_in, core_own, x_out, x_in, x_own, z_out, z_in,
     gz_send, gz_recv, gx_send, gx_recv, gc_send, gc_recv,
     sc_send, sc_recv, sx_send, sx_recv, sz_send, sz_recv, local_sem,
@@ -126,15 +128,20 @@
     z = me // (NX * NC)
     vocab_rows, features = head.shape
     width = features // HALVES
+    gather_width = features // GATHER_HALVES
 
     def index(z_, x_, c_):
         return z_ * (NX * NC) + x_ * NC + c_
 
-    def plane(k):
-        return lax.rem(z + k, NZ)
-
-    def chunk(device):
-        return pl.ds(pl.multiple_of(device * CHUNK, CHUNK), CHUNK)
+    def arrival(j):
+        found = jnp.int32(ARRIVALS[0][j])
+        for i in range(1, NZ):
+            found = jnp.where(z == i, ARRIVALS[i][j], found)
+        return found
+
+    arrived = [z] + [arrival(j) for j in range(1, NZ)]
+    has_below, has_above = z > 0, z < NZ - 1
+    below, above = index(z - 1, x, core), index(z + 1, x, core)
 
     def piece(offset):
         return pl.ds(pl.multiple_of(offset, CHUNK), CHUNK)
@@ -147,88 +154,112 @@
 
     core_peer = index(z, x, 1 - core)
     x_peer = index(z, 1 - x, core)
-    z_peers = [index(plane(k), x, core) for k in range(1, NZ)]
-
-    load_head = pltpu.make_async_copy(weight, head, local_sem.at[0])
-    load_rows = pltpu.make_async_copy(hidden, rows.at[chunk(me)], local_sem.at[1])
+
+    load_rows = pltpu.make_async_copy(hidden, rows.at[piece(me * CHUNK)], local_sem.at[0])
+    load_head = pltpu.make_async_copy(weight, head, local_sem.at[1])
+    small = [
+        pltpu.make_async_copy(source, target, local_sem.at[2 + i])
+        for i, (source, target) in enumerate((
+            (totals, totals_row), (cotangent, cotangent_row), (labels, labels_row),
+            (entry_list, list_held), (entry_valid, valid_held),
+        ))
+    ]
     load_rows.start()
+    for copy in small:
+        copy.start()
     load_head.start()
 
     barrier = pltpu.get_barrier_semaphore()
-    for peer in [core_peer, x_peer] + z_peers:
+
+    def greet(peer):
         pl.semaphore_signal(barrier, inc=1, device_id={"vocab": peer}, device_id_type=MESH)
 
-    for vector, column in (
-        (totals, totals_col), (cotangent, cotangent_col), (labels, labels_col)
-    ):
-        column[...] = jnp.broadcast_to(vector[...], (128, vector.shape[1])).T
+    greet(core_peer)
+    greet(x_peer)
+    pl.when(has_below)(lambda: greet(below))
+    pl.when(has_above)(lambda: greet(above))
 
     load_rows.wait()
-    pl.semaphore_wait(barrier, NZ + 1)
-
-    def gather_copy(source, send, recv, device):
-        held = rows.at[chunk(source)]
-        return remote(held, held, send, recv, device)
-
-    gather_z = {
-        k: gather_copy(me, gz_send.at[k], gz_recv.at[k], index(lax.rem(z + NZ - k, NZ), x, core))
-        for k in range(1, NZ)
-    }
+    pl.semaphore_wait(
+        barrier, 2 + jnp.where(has_below, 1, 0) + jnp.where(has_above, 1, 0)
+    )
+
+    def gather_copy(device, h, send, recv, to):
+        held = rows.at[piece(device * CHUNK), h * gather_width:(h + 1) * gather_width]
+        return remote(held, held, send, recv, to)
+
+    def gather_z(j, h, to, slot):
+        source = arrived[j]
+        return gather_copy(
+            index(source, x, core), h,
+            gz_send.at[slot * GATHER_HALVES + h], gz_recv.at[source * GATHER_HALVES + h], to,
+        )
+
+    def forward_z(j, h, act):
+        if j == 0:
+            pl.when(has_below)(lambda: act(gather_z(0, h, below, 0)))
+            pl.when(has_above)(lambda: act(gather_z(0, h, above, NZ)))
+        else:
+            rising = arrived[j] < z
+            pl.when(rising & has_above)(lambda: act(gather_z(j, h, above, j)))
+            pl.when((arrived[j] > z) & has_below)(lambda: act(gather_z(j, h, below, j)))
+
+    def start(copy):
+        copy.start()
+
+    def sent(copy):
+        copy.wait_send()
+
+    places = [(j, h) for j in range(NZ) for h in range(GATHER_HALVES)]
     gather_x = {
-        k: gather_copy(index(plane(k), x, core), gx_send.at[k], gx_recv.at[k], x_peer)
-        for k in range(NZ)
+        (j, h): gather_copy(
+            index(arrived[j], x, core), h,
+            gx_send.at[j * GATHER_HALVES + h], gx_recv.at[j * GATHER_HALVES + h], x_peer,
+        )
+        for j, h in places
     }
     gather_c = {
-        (k, i): gather_copy(
-            index(plane(k), (x, 1 - x)[i], core), gc_send.at[2 * k + i], gc_recv.at[2 * k + i], core_peer
-        )
-        for k in range(NZ)
+        (j, i, h): gather_copy(
+            index(arrived[j], (x, 1 - x)[i], core), h,
+            gc_send.at[(j * NX + i) * GATHER_HALVES + h], gc_recv.at[(j * NX + i) * GATHER_HALVES + h],
+            core_peer,
+        )
+        for j, h in places
         for i in range(NX)
     }
-    gather_x[0].start()
-    for k in GATHER_ORDER[1:]:
-        gather_z[k].start()
-    gather_c[0, 0].start()
-
-    def dlogits(k):
-        zk = plane(k)
-        span = pl.ds(pl.multiple_of(zk * GROUP, GROUP), GROUP)
-        gather_c[k, 0].wait_recv()
-        gather_c[k, 1].wait_recv()
-        logits = lax.dot_general(
-            rows[span, :], head[...], (((1,), (1,)), ((), ())), preferred_element_type=jnp.float32
-        )
+
+    def add_logits(j, h):
+        span = pl.ds(pl.multiple_of(arrived[j] * GROUP, GROUP), GROUP)
+        here = slice(h * gather_width, (h + 1) * gather_width)
+        for i in range(NX):
+            gather_c[j, i, h].wait_recv()
+        term = lax.dot_general(
+            head[:, here], rows[span, here], (((1,), (1,)), ((), ())),
+            preferred_element_type=jnp.float32,
+        )
+        if h:
+            logits_acc[...] += term
+        else:
+            logits_acc[...] = term
+        if h == GATHER_HALVES - 1:
+            dlogits(j)
+
+    def dlogits(j):
+        span = pl.ds(pl.multiple_of(arrived[j] * GROUP, GROUP), GROUP)
+        logits = logits_acc[...].T
         column = lax.broadcasted_iota(jnp.int32, (1, vocab_rows), 1)
-        token_block = zk * GROUP // TB
+        token_block = arrived[j] * GROUP // TB
         keep = jnp.zeros((1, vocab_rows), jnp.int32)
-        for e in range(entry_valid.shape[0]):
+        for e in range(valid_held.shape[0]):
             used = jnp.where(
-                (entry_list[e, 0] == token_block) & (entry_valid[e] > 0), entry_list[e, 1], -1
+                (list_held[0, e] == token_block) & (valid_held[e] > 0), list_held[1, e], -1
             )
             keep = jnp.where(column // VB == used, 1, keep)
         hit = (labels_col[span, 0:1] == me * vocab_rows + column).astype(jnp.float32)
         value = cotangent_col[span, 0:1] * (jnp.exp(logits - totals_col[span, 0:1]) - hit)
         grad[span, :] = jnp.where(keep > 0, value, 0.0).astype(jnp.bfloat16)
 
-    for i, k in enumerate(GATHER_ORDER):
-        if k:
-            gather_z[k].wait_recv()
-            gather_x[k].start()
-            gather_c[k, 0].start()
-        gather_x[k].wait_recv()
-        gather_c[k, 1].start()
-        if i == 0:
-            load_head.wait()
-        else:
-            dlogits(GATHER_ORDER[i - 1])
-    dlogits(GATHER_ORDER[-1])
-
-    save_rows = pltpu.make_async_copy(rows, gathered_out, local_sem.at[2])
-    save_grad = pltpu.make_async_copy(grad, gradient_out, local_sem.at[3])
-    save_rows.start()
-    save_grad.start()
-
-    steps = [(k, h) for k in SCATTER_ORDER for h in range(HALVES)]
+    steps = [(j, h) for j in SCATTER_ORDER for h in range(HALVES)]
     scatter_c = [
         remote(core_out.at[s], core_in.at[s], sc_send.at[s], sc_recv.at[s], core_peer)
         for s in range(len(steps))
@@ -237,17 +268,10 @@
         remote(x_out.at[s], x_in.at[s], sx_send.at[s], sx_recv.at[s], x_peer)
         for s in range(len(steps))
     ]
-    scatter_z = {
-        s: remote(
-            z_out.at[s], z_in.at[s], sz_send.at[s], sz_recv.at[s], index(plane(k), x, core)
-        )
-        for s, (k, h) in enumerate(steps)
-        if k
-    }
 
     def make_part(s):
-        k, h = steps[s]
-        span = pl.ds(pl.multiple_of(plane(k) * GROUP, GROUP), GROUP)
+        j, h = steps[s]
+        span = pl.ds(pl.multiple_of(arrived[j] * GROUP, GROUP), GROUP)
         part[...] = jnp.dot(
             grad[span, :], head[:, h * width:(h + 1) * width], preferred_element_type=jnp.float32
         )
@@ -264,36 +288,123 @@
         scatter_x[s].start()
         x_own[s] = core_own[s, own, :] + core_in[s, own, :].astype(jnp.float32)
 
+    def z_slot(owner, falling, h):
+        return (owner * 2 + falling) * HALVES + h
+
+    def scatter_z(s, to, falling):
+        j, h = steps[s]
+        slot = z_slot(arrived[j], falling, h)
+        return remote(z_out.at[s], z_in.at[slot], sz_send.at[s], sz_recv.at[slot], to)
+
+    def pass_z(s, act):
+        rises = arrived[steps[s][0]] > z
+        pl.when(rises)(lambda: act(scatter_z(s, above, 0)))
+        pl.when(jnp.logical_not(rises))(lambda: act(scatter_z(s, below, 1)))
+
     def add_x(s):
         scatter_x[s].wait_recv()
         total = x_own[s] + x_in[s].astype(jnp.float32)
-        if s in scatter_z:
-            z_out[s] = total.astype(jnp.bfloat16)
-            scatter_z[s].start()
-        else:
-            x_own[s] = total
-
-    for s in range(len(steps) + 2):
+        x_own[s] = total
+        if steps[s][0]:
+            rises = arrived[steps[s][0]] > z
+
+            @pl.when(jnp.logical_not((rises & has_below) | (jnp.logical_not(rises) & has_above)))
+            def _():
+                z_out[s] = x_own[s].astype(jnp.bfloat16)
+                pass_z(s, start)
+
+    def take_z(s, falling):
+        scatter_z(s, x_peer, falling).wait_recv()
+        slot = z_slot(arrived[steps[s][0]], falling, steps[s][1])
+        x_own[s] += z_in[slot].astype(jnp.float32)
+
+    def add_z(s):
+        rises = arrived[steps[s][0]] > z
+
+        @pl.when(rises & has_below)
+        def _():
+            take_z(s, 0)
+            z_out[s] = x_own[s].astype(jnp.bfloat16)
+            scatter_z(s, above, 0).start()
+
+        @pl.when(jnp.logical_not(rises) & has_above)
+        def _():
+            take_z(s, 1)
+            z_out[s] = x_own[s].astype(jnp.bfloat16)
+            scatter_z(s, below, 1).start()
+
+    for h in range(GATHER_HALVES):
+        gather_x[0, h].start()
+        forward_z(0, h, start)
+    for h in range(GATHER_HALVES):
+        gather_c[0, 0, h].start()
+    for copy in small:
+        copy.wait()
+    for vector, column in (
+        (totals_row, totals_col), (cotangent_row, cotangent_col), (labels_row, labels_col)
+    ):
+        column[...] = jnp.broadcast_to(vector[...], (128, vector.shape[1])).T
+
+    def pass_x(j, h):
+        gather_x[j, h].wait_recv()
+        gather_c[j, 1, h].start()
+
+    waiting = []
+    for j, h in places[GATHER_HALVES:]:
+        gather_z(j, h, x_peer, j).wait_recv()
+        forward_z(j, h, start)
+        gather_x[j, h].start()
+        gather_c[j, 0, h].start()
+        pass_x(j - 1, h)
+        if waiting:
+            if len(waiting) == 1:
+                load_head.wait()
+            add_logits(*waiting[-1])
+        waiting.append((j - 1, h))
+    add_logits(*waiting[-1])
+    for s in range(HALVES):
+        make_part(s)
+    for h in range(GATHER_HALVES):
+        pass_x(NZ - 1, h)
+        if h:
+            add_logits(NZ - 1, h - 1)
+    for s in range(HALVES):
+        add_core(s)
+    add_logits(NZ - 1, GATHER_HALVES - 1)
+
+    save_rows = pltpu.make_async_copy(rows, gathered_out, local_sem.at[7])
+    save_grad = pltpu.make_async_copy(grad, gradient_out, local_sem.at[8])
+
+    passing = len(steps) - HALVES
+    for s in range(HALVES, len(steps) + 4):
         if s < len(steps):
             make_part(s)
-        if 0 <= s - 1 < len(steps):
+        if HALVES <= s - 1 < len(steps):
             add_core(s - 1)
-        if 0 <= s - 2 < len(steps):
+        if s < 2 * HALVES:
+            add_x(s - HALVES)
+        if HALVES <= s - 2 < len(steps):
             add_x(s - 2)
+        if HALVES <= s - 4 < passing:
+            add_z(s - 4)
+        if s == len(steps):
+            save_rows.start()
+            save_grad.start()
+    for s in range(HALVES):
+        add_z(s)
 
     for h in range(HALVES):
-        total = x_own[steps.index((0, h))]
-        for s, (k, half) in enumerate(steps):
-            if k and half == h:
-                scatter_z[s].wait_recv()
-                total = total + z_in[s].astype(jnp.float32)
-        grad_hidden[:, h * width:(h + 1) * width] = total.astype(jnp.bfloat16)
-
-    for copy in (
-        list(gather_z.values()) + list(gather_x.values()) + list(gather_c.values())
-        + scatter_c + scatter_x + list(scatter_z.values())
-    ):
+        s = passing + h
+        pl.when(has_below)(lambda: take_z(s, 0))
+        pl.when(has_above)(lambda: take_z(s, 1))
+        grad_hidden[:, h * width:(h + 1) * width] = x_own[s].astype(jnp.bfloat16)
+
+    for j, h in places:
+        forward_z(j, h, sent)
+    for copy in list(gather_x.values()) + list(gather_c.values()) + scatter_c + scatter_x:
         copy.wait_send()
+    for s in range(passing):
+        pass_z(s, sent)
     save_rows.wait()
     save_grad.wait()
 
@@ -301,12 +412,12 @@
 def local_fused(hidden, weight, log_totals, token_cotangent, targets, block_list, block_valid):
     tokens = log_totals.shape[0]
     vocab_rows, features = weight.shape
+    entries = block_valid.shape[0]
     width = features // HALVES
     steps = NZ * HALVES
-    bf16, f32 = jnp.bfloat16, jnp.float32
-    vmem = pl.BlockSpec(memory_space=pltpu.VMEM)
-    smem = pl.BlockSpec(memory_space=pltpu.SMEM)
-    hbm = pl.BlockSpec(memory_space=pl.ANY)
+    places = NZ * GATHER_HALVES
+    bf16, f32, i32 = jnp.bfloat16, jnp.float32, jnp.int32
+    hbm = pl.BlockSpec(memory_space=pltpu.HBM)
     dma = pltpu.SemaphoreType.DMA
     grad_hidden, gradient, gathered = pl.pallas_call(
         head_kernel,
@@ -315,16 +426,26 @@
             jax.ShapeDtypeStruct((tokens, vocab_rows), bf16),
             jax.ShapeDtypeStruct((tokens, features), bf16),
         ),
-        in_specs=[hbm, hbm, vmem, vmem, vmem, smem, smem],
-        out_specs=(vmem, hbm, hbm),
+        in_specs=[hbm] * 7,
+        out_specs=(
+            pl.BlockSpec(memory_space=pltpu.VMEM),
+            pl.BlockSpec(memory_space=pl.ANY),
+            pl.BlockSpec(memory_space=pl.ANY),
+        ),
         scratch_shapes=[
             pltpu.VMEM((tokens, features), bf16),
             pltpu.VMEM((vocab_rows, features), bf16),
             pltpu.VMEM((tokens, vocab_rows), bf16),
             pltpu.VMEM((GROUP, width), f32),
+            pltpu.VMEM((1, tokens), f32),
+            pltpu.VMEM((1, tokens), f32),
+            pltpu.VMEM((1, tokens), i32),
+            pltpu.SMEM((2, entries), i32),
+            pltpu.SMEM((entries,), i32),
             pltpu.VMEM((tokens, 128), f32),
             pltpu.VMEM((tokens, 128), f32),
-            pltpu.VMEM((tokens, 128), jnp.int32),
+            pltpu.VMEM((tokens, 128), i32),
+            pltpu.VMEM((vocab_rows, GROUP), f32),
             pltpu.VMEM((steps, NX * CHUNK, width), bf16),
             pltpu.VMEM((steps, NX * CHUNK, width), bf16),
             pltpu.VMEM((steps, NX * CHUNK, width), f32),
@@ -332,17 +453,19 @@
             pltpu.VMEM((steps, CHUNK, width), bf16),
             pltpu.VMEM((steps, CHUNK, width), f32),
             pltpu.VMEM((steps, CHUNK, width), bf16),
-            pltpu.VMEM((steps, CHUNK, width), bf16),
-            dma((NZ,)), dma((NZ,)), dma((NZ,)), dma((NZ,)), dma((2 * NZ,)), dma((2 * NZ,)),
-            dma((steps,)), dma((steps,)), dma((steps,)), dma((steps,)), dma((steps,)), dma((steps,)),
-            dma((4,)),
+            pltpu.VMEM((2 * steps, CHUNK, width), bf16),
+            dma((places + GATHER_HALVES,)), dma((places,)),
+            dma((places,)), dma((places,)), dma((2 * places,)), dma((2 * places,)),
+            dma((steps,)), dma((steps,)), dma((steps,)), dma((steps,)),
+            dma((steps,)), dma((2 * steps,)),
+            dma((9,)),
         ],
         compiler_params=pltpu.CompilerParams(
-            collective_id=0, has_side_effects=True, vmem_limit_bytes=48 * 1024 * 1024
+            collective_id=0, has_side_effects=True, vmem_limit_bytes=64 * 1024 * 1024
         ),
     )(
         hidden, weight, log_totals[None, :], token_cotangent[None, :], targets[None, :],
-        block_list, block_valid,
+        block_list.T, block_valid,
     )
     grad_weight = lax.dot_general(
         gradient, gathered, (((0,), (0,)), ((), ())), preferred_element_type=f32

time: 65.7 us -> 56.3 us (0.86)
  Pallas kernels: 56.2 us -> 49.5 us
  local copies, waits for them, and re-layouts: 5.03 us -> 0.67 us
  matrix products: 3.61 us -> 5.4 us
    pallas_call x1, Pallas kernels: 56.2 us -> 49.5 us  [local_fused(): pl.pallas_call(head_kernel, out_shape=(jax.ShapeDtypeStruct(hidden.shape,...]
    unnamed x12 -> x3, local copies, waits for them, and re-layouts: 5.03 us -> 0.67 us
    dot_general x1, matrix products: 3.61 us -> 5.4 us  [local_fused(): lax.dot_general(gradient, gathered, (((0,), (0,)), ((), ())), preferred_e...]
where the time goes in v2:
time: 56.3 us; the launch traced here: 56.2 us
  Pallas kernels  49.5 us (88%)
  matrix products  5.4 us (10%)
  local copies, waits for them, and re-layouts  0.67 us (1%)
  between operations  0.65 us (1%)
    pallas_call x1, Pallas kernels, local_fused(): pl.pallas_call(head_kernel, out_shape=(jax.ShapeDtypeStruct(hidden.shape,...  49.5 us
    dot_general x1, matrix products, local_fused(): lax.dot_general(gradient, gathered, (((0,), (0,)), ((), ())), preferred_e...  5.4 us

profile of v2, /device:TPU:0, one launch (start us, length us, event | category | flops | bytes accessed | tf_op | source)
XLA Modules:
  0.0 56.2 jit_solution(3237578132567080881)
XLA Ops:
  0.6 49.5 %shard_map.86 = (bf16[16,4608]{1,0:T(8,128)(2,1)}, bf16[256,512]{1,0:T(8,128)(2,1)}, bf16[256,4608]{1,0:T(8,128)(2,1)}) custom-call(bf16[16,4608]{1,0:T(8,128)(2,1)} %hidden.1, bf16[512,4608]{1,0:T(8,128)(2,1)} %weight.1, f32[1,256]{1,0:T(1,128)} %bitcast.6, f32[1,256]{1,0:T(1,128)} %bitcast.7, s32[1,256]{1,0:T(1,128)} %bitcast.8, s32[2,4]{1,0:T(2,128)} %bitcast.9, ...), custom_call_target="tpu_custom_call" | custom-call | tf_op jit(solution)/shard_map/pallas_call | solution.py:422
  50.1 0.0 copy-start
  50.1 5.4 %convolution_convert_fusion = bf16[512,4608]{1,0:T(8,128)(2,1)} fusion(bf16[256,512]{1,0:T(8,128)(2,1)} %get-tuple-element.6, bf16[256,4608]{1,0:T(8,128)(2,1)} %get-tuple-element.7), kind=kOutput, calls=%fused_computation | convolution fusion | flops 1210318848 | bytes 7340032 | tf_op jit(solution)/shard_map/dot_general | solution.py:470
  55.5 0.0 copy-done
  55.5 0.7 %copy.10 = bf16[16,4608]{1,0:T(8,128)(2,1)} copy(bf16[16,4608]{1,0:T(8,128)(2,1)S(1)} %copy-done) | data formatting | bytes 294912
Async XLA Ops:
  50.1 5.4 %copy-start = (bf16[16,4608]{1,0:T(8,128)(2,1)S(1)}, bf16[16,4608]{1,0:T(8,128)(2,1)}, u32[]{:S(2)}) copy-start(bf16[16,4608]{1,0:T(8,128)(2,1)} %get-tuple-element.10) | copy-start | bytes 442372

commit v3 on v2

--- a/solution.py
+++ b/solution.py
@@ -176,13 +176,11 @@
 
     greet(core_peer)
     greet(x_peer)
-    pl.when(has_below)(lambda: greet(below))
-    pl.when(has_above)(lambda: greet(above))
+    for k in range(1, NZ):
+        greet(index(lax.rem(z + k, NZ), x, core))
 
     load_rows.wait()
-    pl.semaphore_wait(
-        barrier, 2 + jnp.where(has_below, 1, 0) + jnp.where(has_above, 1, 0)
-    )
+    pl.semaphore_wait(barrier, NZ + 1)
 
     def gather_copy(device, h, send, recv, to):
         held = rows.at[piece(device * CHUNK), h * gather_width:(h + 1) * gather_width]
@@ -288,50 +286,22 @@
         scatter_x[s].start()
         x_own[s] = core_own[s, own, :] + core_in[s, own, :].astype(jnp.float32)
 
-    def z_slot(owner, falling, h):
-        return (owner * 2 + falling) * HALVES + h
-
-    def scatter_z(s, to, falling):
+    def scatter_z(s, source):
         j, h = steps[s]
-        slot = z_slot(arrived[j], falling, h)
-        return remote(z_out.at[s], z_in.at[slot], sz_send.at[s], sz_recv.at[slot], to)
-
-    def pass_z(s, act):
-        rises = arrived[steps[s][0]] > z
-        pl.when(rises)(lambda: act(scatter_z(s, above, 0)))
-        pl.when(jnp.logical_not(rises))(lambda: act(scatter_z(s, below, 1)))
+        slot = source * HALVES + h
+        return remote(
+            z_out.at[s], z_in.at[slot], sz_send.at[s], sz_recv.at[slot],
+            index(arrived[j], x, core),
+        )
 
     def add_x(s):
         scatter_x[s].wait_recv()
         total = x_own[s] + x_in[s].astype(jnp.float32)
-        x_own[s] = total
         if steps[s][0]:
-            rises = arrived[steps[s][0]] > z
-
-            @pl.when(jnp.logical_not((rises & has_below) | (jnp.logical_not(rises) & has_above)))
-            def _():
-                z_out[s] = x_own[s].astype(jnp.bfloat16)
-                pass_z(s, start)
-
-    def take_z(s, falling):
-        scatter_z(s, x_peer, falling).wait_recv()
-        slot = z_slot(arrived[steps[s][0]], falling, steps[s][1])
-        x_own[s] += z_in[slot].astype(jnp.float32)
-
-    def add_z(s):
-        rises = arrived[steps[s][0]] > z
-
-        @pl.when(rises & has_below)
-        def _():
-            take_z(s, 0)
-            z_out[s] = x_own[s].astype(jnp.bfloat16)
-            scatter_z(s, above, 0).start()
-
-        @pl.when(jnp.logical_not(rises) & has_above)
-        def _():
-            take_z(s, 1)
-            z_out[s] = x_own[s].astype(jnp.bfloat16)
-            scatter_z(s, below, 1).start()
+            z_out[s] = total.astype(jnp.bfloat16)
+            scatter_z(s, z).start()
+        else:
+            x_own[s] = total
 
     for h in range(GATHER_HALVES):
         gather_x[0, h].start()
@@ -376,7 +346,7 @@
     save_grad = pltpu.make_async_copy(grad, gradient_out, local_sem.at[8])
 
     passing = len(steps) - HALVES
-    for s in range(HALVES, len(steps) + 4):
+    for s in range(HALVES, len(steps) + 2):
         if s < len(steps):
             make_part(s)
         if HALVES <= s - 1 < len(steps):
@@ -385,26 +355,23 @@
             add_x(s - HALVES)
         if HALVES <= s - 2 < len(steps):
             add_x(s - 2)
-        if HALVES <= s - 4 < passing:
-            add_z(s - 4)
         if s == len(steps):
             save_rows.start()
             save_grad.start()
-    for s in range(HALVES):
-        add_z(s)
 
     for h in range(HALVES):
-        s = passing + h
-        pl.when(has_below)(lambda: take_z(s, 0))
-        pl.when(has_above)(lambda: take_z(s, 1))
-        grad_hidden[:, h * width:(h + 1) * width] = x_own[s].astype(jnp.bfloat16)
+        total = x_own[passing + h]
+        for j in range(1, NZ):
+            scatter_z(steps.index((j, h)), arrived[j]).wait_recv()
+            total = total + z_in[arrived[j] * HALVES + h].astype(jnp.float32)
+        grad_hidden[:, h * width:(h + 1) * width] = total.astype(jnp.bfloat16)
 
     for j, h in places:
         forward_z(j, h, sent)
     for copy in list(gather_x.values()) + list(gather_c.values()) + scatter_c + scatter_x:
         copy.wait_send()
     for s in range(passing):
-        pass_z(s, sent)
+        scatter_z(s, z).wait_send()
     save_rows.wait()
     save_grad.wait()
 
@@ -453,11 +420,11 @@
             pltpu.VMEM((steps, CHUNK, width), bf16),
             pltpu.VMEM((steps, CHUNK, width), f32),
             pltpu.VMEM((steps, CHUNK, width), bf16),
-            pltpu.VMEM((2 * steps, CHUNK, width), bf16),
+            pltpu.VMEM((steps, CHUNK, width), bf16),
             dma((places + GATHER_HALVES,)), dma((places,)),
             dma((places,)), dma((places,)), dma((2 * places,)), dma((2 * places,)),
             dma((steps,)), dma((steps,)), dma((steps,)), dma((steps,)),
-            dma((steps,)), dma((2 * steps,)),
+            dma((steps,)), dma((steps,)),
             dma((9,)),
         ],
         compiler_params=pltpu.CompilerParams(

time: 56.3 us -> 53.4 us (0.948)
  Pallas kernels: 49.5 us -> 46.5 us
    pallas_call x1, Pallas kernels: 49.5 us -> 46.5 us  [local_fused(): pl.pallas_call(head_kernel, out_shape=(jax.ShapeDtypeStruct(hidden.shape,...]
where the time goes in v3:
time: 53.4 us; the launch traced here: 53.3 us
  Pallas kernels  46.5 us (87%)
  matrix products  5.4 us (10%)
  local copies, waits for them, and re-layouts  0.67 us (1%)
  between operations  0.65 us (1%)
    pallas_call x1, Pallas kernels, local_fused(): pl.pallas_call(head_kernel, out_shape=(jax.ShapeDtypeStruct(hidden.shape,...  46.5 us
    dot_general x1, matrix products, local_fused(): lax.dot_general(gradient, gathered, (((0,), (0,)), ((), ())), preferred_e...  5.4 us

profile of v3, /device:TPU:0, one launch (start us, length us, event | category | flops | bytes accessed | tf_op | source)
XLA Modules:
  0.0 53.3 jit_solution(12489738368572146251)
XLA Ops:
  0.6 46.5 %shard_map.86 = (bf16[16,4608]{1,0:T(8,128)(2,1)}, bf16[256,512]{1,0:T(8,128)(2,1)}, bf16[256,4608]{1,0:T(8,128)(2,1)}) custom-call(bf16[16,4608]{1,0:T(8,128)(2,1)} %hidden.1, bf16[512,4608]{1,0:T(8,128)(2,1)} %weight.1, f32[1,256]{1,0:T(1,128)} %bitcast.6, f32[1,256]{1,0:T(1,128)} %bitcast.7, s32[1,256]{1,0:T(1,128)} %bitcast.8, s32[2,4]{1,0:T(2,128)} %bitcast.9, ...), custom_call_target="tpu_custom_call" | custom-call | tf_op jit(solution)/shard_map/pallas_call | solution.py:389
  47.2 0.0 copy-start
  47.2 5.4 %convolution_convert_fusion = bf16[512,4608]{1,0:T(8,128)(2,1)} fusion(bf16[256,512]{1,0:T(8,128)(2,1)} %get-tuple-element.6, bf16[256,4608]{1,0:T(8,128)(2,1)} %get-tuple-element.7), kind=kOutput, calls=%fused_computation | convolution fusion | flops 1210318848 | bytes 7340032 | tf_op jit(solution)/shard_map/dot_general | solution.py:437
  52.6 0.0 copy-done
  52.6 0.7 %copy.10 = bf16[16,4608]{1,0:T(8,128)(2,1)} copy(bf16[16,4608]{1,0:T(8,128)(2,1)S(1)} %copy-done) | data formatting | bytes 294912
Async XLA Ops:
  47.2 5.4 %copy-start = (bf16[16,4608]{1,0:T(8,128)(2,1)S(1)}, bf16[16,4608]{1,0:T(8,128)(2,1)}, u32[]{:S(2)}) copy-start(bf16[16,4608]{1,0:T(8,128)(2,1)} %get-tuple-element.10) | copy-start | bytes 442372

commit v4 on v3

--- a/solution.py
+++ b/solution.py
@@ -346,15 +346,15 @@
     save_grad = pltpu.make_async_copy(grad, gradient_out, local_sem.at[8])
 
     passing = len(steps) - HALVES
-    for s in range(HALVES, len(steps) + 2):
+    for s in range(HALVES, len(steps) + 3):
         if s < len(steps):
             make_part(s)
         if HALVES <= s - 1 < len(steps):
             add_core(s - 1)
         if s < 2 * HALVES:
             add_x(s - HALVES)
-        if HALVES <= s - 2 < len(steps):
-            add_x(s - 2)
+        if HALVES <= s - 3 < len(steps):
+            add_x(s - 3)
         if s == len(steps):
             save_rows.start()
             save_grad.start()

time: 53.4 us -> 52.1 us (0.976)
  Pallas kernels: 46.5 us -> 45.3 us
    pallas_call x1, Pallas kernels: 46.5 us -> 45.3 us  [local_fused(): pl.pallas_call(head_kernel, out_shape=(jax.ShapeDtypeStruct(hidden.shape,...]
where the time goes in v4:
time: 52.1 us; the launch traced here: 52 us
  Pallas kernels  45.3 us (87%)
  matrix products  5.4 us (10%)
  local copies, waits for them, and re-layouts  0.67 us (1%)
  between operations  0.65 us (1%)
    pallas_call x1, Pallas kernels, local_fused(): pl.pallas_call(head_kernel, out_shape=(jax.ShapeDtypeStruct(hidden.shape,...  45.3 us
    dot_general x1, matrix products, local_fused(): lax.dot_general(gradient, gathered, (((0,), (0,)), ((), ())), preferred_e...  5.4 us

profile of v4, /device:TPU:0, one launch (start us, length us, event | category | flops | bytes accessed | tf_op | source)
XLA Modules:
  0.0 52.0 jit_solution(12894902733732717956)
XLA Ops:
  0.6 45.3 %shard_map.86 = (bf16[16,4608]{1,0:T(8,128)(2,1)}, bf16[256,512]{1,0:T(8,128)(2,1)}, bf16[256,4608]{1,0:T(8,128)(2,1)}) custom-call(bf16[16,4608]{1,0:T(8,128)(2,1)} %hidden.1, bf16[512,4608]{1,0:T(8,128)(2,1)} %weight.1, f32[1,256]{1,0:T(1,128)} %bitcast.6, f32[1,256]{1,0:T(1,128)} %bitcast.7, s32[1,256]{1,0:T(1,128)} %bitcast.8, s32[2,4]{1,0:T(2,128)} %bitcast.9, ...), custom_call_target="tpu_custom_call" | custom-call | tf_op jit(solution)/shard_map/pallas_call | solution.py:389
  45.9 0.0 copy-start
  45.9 5.4 %convolution_convert_fusion = bf16[512,4608]{1,0:T(8,128)(2,1)} fusion(bf16[256,512]{1,0:T(8,128)(2,1)} %get-tuple-element.6, bf16[256,4608]{1,0:T(8,128)(2,1)} %get-tuple-element.7), kind=kOutput, calls=%fused_computation | convolution fusion | flops 1210318848 | bytes 7340032 | tf_op jit(solution)/shard_map/dot_general | solution.py:437
  51.3 0.0 copy-done
  51.3 0.7 %copy.10 = bf16[16,4608]{1,0:T(8,128)(2,1)} copy(bf16[16,4608]{1,0:T(8,128)(2,1)S(1)} %copy-done) | data formatting | bytes 294912
Async XLA Ops:
  45.9 5.4 %copy-start = (bf16[16,4608]{1,0:T(8,128)(2,1)S(1)}, bf16[16,4608]{1,0:T(8,128)(2,1)}, u32[]{:S(2)}) copy-start(bf16[16,4608]{1,0:T(8,128)(2,1)} %get-tuple-element.10) | copy-start | bytes 442372
